TPU v7x, 256 devices: a whole 4x4x8 slice. The times are simulated.
256 devices in a mesh: ctx: 32 (over y, x, z_hi), head: 8 (over z_lo, core).
Axes of the slice: x: 4, y: 4, z: 8 (z_hi: 2, z_lo: 4; z = z_hi * 4 + z_lo), core: 2. Of those that a mesh axis runs over, the one named last changes fastest.
Arguments:
- queries: bfloat16 [32768, 2048], P('ctx', 'head'), may hold values from -8 to 8
- keys: bfloat16 [32768, 2048], P('ctx', 'head'), may hold values from -8 to 8
- values: bfloat16 [32768, 2048], P('ctx', 'head'), may hold values from -6 to 6
- rates: float32 [32768, 8], P('ctx', 'head'), may hold values from 2 to 32
- doc_ids: int32 [32768], P('ctx'), may hold values from 0 to 15, never falling along the last dimension, each value on 1 to 4096 neighbouring positions
- windows: int32 [8], P('head'), may hold values from 256 to 1024, as said below
- fast_weights: float32 [3, 8, 256, 768], P(None, 'head', None, 'ctx'), may hold values from -0.375 to 0.375
- momentum: float32 [3, 8, 256, 768], P(None, 'head', None, 'ctx'), may hold values from -0.06 to 0.06
- out_gain: float32 [8, 256], P('head'), may hold values from 0.25 to 1.75
Outputs:
- mixed: bfloat16 [32768, 2048], P('ctx', 'head')
- new_weights: float32 [3, 8, 256, 768], P(None, 'head', None, 'ctx')
- new_momentum: float32 [3, 8, 256, 768], P(None, 'head', None, 'ctx')
Inputs may be any that keep to these rules, and one draw needn't show every extreme that they name: `windows`: one head's window is exactly 1024.
All inputs are finite; a program needn't handle non-finite values.
Results may differ from a plain program's by a relative error of at most 0.022.
Values may be sent and summed in bfloat16 or wider, within the bound.
A program may use at most 64 MiB of HBM per device.

v0:
```python
import jax
import jax.numpy as jnp
from jax import lax
from jax.sharding import PartitionSpec as P

DH = 256
WIN = 1024


def from_behind(block, axis, distance):
    devices = range(lax.axis_size(axis))
    route = [(i - distance, i) for i in devices if i - distance in devices]
    return lax.ppermute(block, axis, route)


def silu_pair(gate_part):
    sigma = jax.nn.sigmoid(gate_part)
    return (gate_part * sigma, sigma * (1.0 + gate_part * (1.0 - sigma)))


def fast_update(key_rows, value_rows, rate_rows, old_bf, token_count):
    gate_part = jnp.dot(key_rows, old_bf[0], preferred_element_type=jnp.float32)
    up_part = jnp.dot(key_rows, old_bf[1], preferred_element_type=jnp.float32)
    active, slope = silu_pair(gate_part)
    hidden = (active * up_part).astype(jnp.bfloat16)
    d_pred = (-(rate_rows / token_count)[:, None] * value_rows.astype(jnp.float32)).astype(
        jnp.bfloat16
    )
    d_hidden = jnp.dot(d_pred, old_bf[2], preferred_element_type=jnp.float32)
    d_gate = (d_hidden * up_part * slope).astype(jnp.bfloat16)
    d_up = (d_hidden * active).astype(jnp.bfloat16)
    contract = (((0,), (0,)), ((), ()))
    return jnp.stack(
        [
            lax.dot_general(key_rows, d_gate, contract, preferred_element_type=jnp.float32),
            lax.dot_general(key_rows, d_up, contract, preferred_element_type=jnp.float32),
            lax.dot_general(d_pred, hidden, contract, preferred_element_type=jnp.float32),
        ]
    )


def renorm(weights, moment, grad):
    new_moment = 0.9 * moment + grad
    stepped = weights - new_moment
    factor = jnp.sqrt(jnp.mean(weights * weights, axis=-2, keepdims=True)) / jnp.sqrt(
        jnp.mean(stepped * stepped, axis=-2, keepdims=True) + 1e-06
    )
    return (stepped * factor, new_moment)


def fast_apply(query_rows, new_bf, gain_row):
    gate_part = jnp.dot(query_rows, new_bf[0], preferred_element_type=jnp.float32)
    up_part = jnp.dot(query_rows, new_bf[1], preferred_element_type=jnp.float32)
    hidden = (silu_pair(gate_part)[0] * up_part).astype(jnp.bfloat16)
    fast_out = lax.dot_general(
        hidden, new_bf[2], (((1,), (1,)), ((), ())), preferred_element_type=jnp.float32
    )
    return (
        fast_out
        * lax.rsqrt(jnp.mean(fast_out * fast_out, axis=-1, keepdims=True) + 1e-06)
        * gain_row
    )


def attend_block(
    query_block, key_block, value_block, query_docs, key_docs, query_pos, key_pos, window
):
    scores = lax.dot_general(
        query_block, key_block, (((1,), (1,)), ((), ())), preferred_element_type=jnp.float32
    ) * query_block.shape[1] ** (-0.5)
    allowed = (key_pos[None, :] >= 0) & (key_pos[None, :] <= query_pos[:, None])
    allowed = allowed & (key_pos[None, :] > query_pos[:, None] - window)
    allowed = allowed & (key_docs[None, :] == query_docs[:, None])
    scores = jnp.where(allowed, scores, -1e30)
    top = jnp.max(scores, axis=-1, keepdims=True)
    expo = jnp.where(allowed, jnp.exp(scores - top), 0.0)
    attn_weights = (expo / jnp.sum(expo, axis=-1, keepdims=True)).astype(jnp.bfloat16)
    return jnp.dot(attn_weights, value_block, preferred_element_type=jnp.float32)


def local(queries, keys, values, rates, doc_ids, windows, fast_weights, momentum, out_gain):
    tok_rows = queries.shape[0]
    token_count = tok_rows * lax.axis_size("ctx")
    own_first = lax.axis_index("ctx") * tok_rows
    hid_share = fast_weights.shape[3]
    full_weights, full_moment = (
        lax.all_gather(fast_weights.astype(jnp.bfloat16), "ctx", axis=3, tiled=True).astype(
            fast_weights.dtype
        ),
        lax.all_gather(momentum.astype(jnp.bfloat16), "ctx", axis=3, tiled=True).astype(
            momentum.dtype
        ),
    )
    old_bf = full_weights.astype(jnp.bfloat16)
    shifts = -(-WIN // tok_rows)
    pieces = [from_behind((keys, values, doc_ids), "ctx", 1)]
    key_buffer = jnp.concatenate([piece[0] for piece in pieces] + [keys], axis=0)
    value_buffer = jnp.concatenate([piece[1] for piece in pieces] + [values], axis=0)
    doc_buffer = jnp.concatenate([piece[2] for piece in pieces] + [doc_ids], axis=0)
    head_num = 0
    grads = [fast_update(keys, values, rates[:, head_num], old_bf[:, head_num], token_count)]
    grad = jnp.stack(grads, axis=1)
    total = lax.psum(grad, "ctx")
    whole_w, whole_m = renorm(full_weights, full_moment, total)
    new_bf = whole_w.astype(jnp.bfloat16)
    col_first = lax.axis_index("ctx") * hid_share
    new_weights = lax.dynamic_slice_in_dim(whole_w, col_first, hid_share, 3)
    new_moment = lax.dynamic_slice_in_dim(whole_m, col_first, hid_share, 3)
    block_rows = min(512, tok_rows)
    head_num = 0
    low_col = head_num * DH
    normed = fast_apply(queries, new_bf[:, head_num], out_gain[head_num])
    blocks = []
    for block_num in range(tok_rows // block_rows):
        first = block_num * block_rows
        begin = shifts * tok_rows + first - WIN
        query_pos = own_first + first + jnp.arange(block_rows, dtype=jnp.int32)
        key_pos = own_first + first - WIN + jnp.arange(WIN + block_rows, dtype=jnp.int32)
        blocks.append(
            attend_block(
                queries[first : first + block_rows],
                key_buffer[begin : begin + WIN + block_rows, low_col : low_col + DH],
                value_buffer[begin : begin + WIN + block_rows, low_col : low_col + DH],
                doc_ids[first : first + block_rows],
                doc_buffer[begin : begin + WIN + block_rows],
                query_pos,
                key_pos,
                windows[head_num],
            )
        )
    attended = jnp.concatenate(blocks, axis=0)
    columns = (attended + normed).astype(jnp.bfloat16)
    return (columns, new_weights, new_moment)


def solution(mesh):
    in_specs = (
        P("ctx", "head"),
        P("ctx", "head"),
        P("ctx", "head"),
        P("ctx", "head"),
        P("ctx"),
        P("head"),
        P(None, "head", None, "ctx"),
        P(None, "head", None, "ctx"),
        P("head", None),
    )
    out_specs = (P("ctx", "head"), P(None, "head", None, "ctx"), P(None, "head", None, "ctx"))
    return jax.shard_map(local, mesh=mesh, in_specs=in_specs, out_specs=out_specs, check_vma=False)
```

profile of v0, /device:TPU:64, one launch (start us, length us, event | category | flops | bytes accessed | tf_op | source)
XLA Modules:
  0.0 663.8 jit_solution(285570956269833204)
XLA Ops:
  7.2 1.5 bitcast_convert_fusion.1
  8.8 7.3 %collective-permute-start = (s32[1024]{0:T(1024)}, s32[1024]{0:T(1024)S(1)}, u32[]{:S(2)}, u32[]{:S(2)}) collective-permute-start(s32[1024]{0:T(1024)} %param.13), channel_id=1, source_target_pairs={{0,8},{8,16},{16,24},{24,32},{32,40},{40,48},{48,56},{56,64},{64,7... | collective-permute-start | bytes 12296 | tf_op jit(solution)/shard_map/ppermute | solution.py:13
  16.1 3.4 collective-permute-start.1
  19.5 7.3 %collective-permute-start.2 = (bf16[1024,256]{1,0:T(8,128)(2,1)}, bf16[1024,256]{1,0:T(8,128)(2,1)S(1)}, u32[]{:S(2)}, u32[]{:S(2)}) collective-permute-start(bf16[1024,256]{1,0:T(8,128)(2,1)} %param.11), channel_id=1, source_target_pairs={{0,8},{8,16},{16,24},{24,32},{32,40},{40,48},{48,56},{56,64},{64,7... | collective-permute-start | bytes 1572872 | tf_op jit(solution)/shard_map/ppermute | solution.py:13
  26.8 1.5 bitcast_convert_fusion
  28.4 0.8 fusion.44
  29.2 0.7 multiply_negate_fusion
  30.6 0.7 constant_dynamic-update-slice_fusion.5
  31.3 22.2 %collective-permute-done.1 = bf16[1024,256]{1,0:T(8,128)(2,1)S(1)} collective-permute-done((bf16[1024,256]{1,0:T(8,128)(2,1)}, bf16[1024,256]{1,0:T(8,128)(2,1)S(1)}, u32[]{:S(2)}, u32[]{:S(2)}) %collective-permute-start.1) | collective-permute-done | bytes 524320 | tf_op jit(solution)/shard_map/ppermute | solution.py:13
  53.6 1.1 constant_dynamic-update-slice_fusion.1
  54.7 4.4 fusion.45
  59.1 3.4 fusion.46
  62.5 51.5 %all-gather.3.cloned.1.call-done = bf16[3,1,256,768]{2,3,0,1:T(8,128)(2,1)} async-done(((bf16[3,1,256,24]{2,3,0,1:T(8,128)(2,1)}), bf16[3,1,256,768]{2,3,0,1:T(8,128)(2,1)}) %all-gather.3.cloned.1.call-update) | async-done | bytes 1179664 | tf_op jit(solution)/shard_map/all_gather | solution.py:87
  114.0 1.7 fusion.30
  116.3 0.6 fusion.32
  117.0 1.1 fusion.21
  118.0 1.6 fusion.19
  119.6 1.3 fusion.20
  120.9 1.6 maximum_bitcast_fusion
  122.7 7.3 %fusion.10 = (f32[512]{0:T(512)S(1)}, f32[512]{0:T(512)S(1)}) fusion(f32[512,1536]{0,1:T(8,128)} %get-tuple-element.18, f32[512]{0:T(512)S(1)} %get-tuple-element.17, s32[512]{0:T(512)S(1)} %get-tuple-element.13, s32[1536]{0:T(1024)S(1)} %get-tuple-element.11, s32[512]{0:T(512)S(1)} %broadcast_subtract_fusion.1, s32[512]{0:T(512)S(1)} %iota_add_fusion.3, ...), kind=kLoop, calls=%fused_computation.30 | loop fusion | flops 14154752 | bytes 6339584 | tf_op jit(solution)/shard_map/reduce_sum | solution.py:77
  130.1 2.9 fusion.15
  132.9 2.9 fusion.16
  135.8 58.5 %all-gather.5.cloned.1.call-done = bf16[3,1,256,768]{2,3,0,1:T(8,128)(2,1)} async-done(((bf16[3,1,256,24]{2,3,0,1:T(8,128)(2,1)}), bf16[3,1,256,768]{2,3,0,1:T(8,128)(2,1)}) %all-gather.5.cloned.1.call-update) | async-done | bytes 1179664 | tf_op jit(solution)/shard_map/all_gather | solution.py:90
  194.4 445.3 %all-reduce.2.cloned.1.call-done = f32[3,1,256,768]{2,3,0,1:T(8,128)} async-done(((f32[3,1,256,768]{2,3,0,1:T(8,128)}), f32[3,1,256,768]{2,3,0,1:T(8,128)}) %all-reduce.2.cloned.1.call-update) | async-done | bytes 2359312 | tf_op jit(solution)/shard_map/psum | solution.py:103
  639.7 2.8 fusion.9
  642.5 1.8 fusion.41
  644.4 1.0 copy-done.4
  645.4 2.3 fusion.29
  647.7 4.2 multiply_reduce_fusion.1
  651.9 1.6 copy.16
  653.5 1.6 dynamic-slice_bitcast_fusion
  655.0 2.2 fusion.22
  (43 shorter events, 1.0 us)
Async XLA Ops:
  7.2 106.8 %all-gather.3.cloned.1.call-start = ((), (), s32[]{:S(2)}) async-start(), calls=%async_computation | async-start | bytes 1216512 | tf_op jit(solution)/shard_map/all_gather | solution.py:87
  8.7 185.6 %all-gather.5.cloned.1.call-start = ((), (), s32[]{:S(2)}) async-start(), calls=%async_computation.1 | async-start | bytes 1216512 | tf_op jit(solution)/shard_map/all_gather | solution.py:90
  8.8 21.8 %collective-permute-start = (s32[1024]{0:T(1024)}, s32[1024]{0:T(1024)S(1)}, u32[]{:S(2)}, u32[]{:S(2)}) collective-permute-start(s32[1024]{0:T(1024)} %param.13), channel_id=1, source_target_pairs={{0,8},{8,16},{16,24},{24,32},{32,40},{40,48},{48,56},{56,64},{64,7... | collective-permute-start | bytes 12296 | tf_op jit(solution)/shard_map/ppermute | solution.py:13
  16.1 37.5 %collective-permute-start.1 = (bf16[1024,256]{1,0:T(8,128)(2,1)}, bf16[1024,256]{1,0:T(8,128)(2,1)S(1)}, u32[]{:S(2)}, u32[]{:S(2)}) collective-permute-start(bf16[1024,256]{1,0:T(8,128)(2,1)} %param.10), channel_id=1, source_target_pairs={{0,8},{8,16},{16,24},{24,32},{32,40},{40,48},{48,56},{56,64},{64,7... | collective-permute-start | bytes 1572872 | tf_op jit(solution)/shard_map/ppermute | solution.py:13
  19.5 103.1 %collective-permute-start.2 = (bf16[1024,256]{1,0:T(8,128)(2,1)}, bf16[1024,256]{1,0:T(8,128)(2,1)S(1)}, u32[]{:S(2)}, u32[]{:S(2)}) collective-permute-start(bf16[1024,256]{1,0:T(8,128)(2,1)} %param.11), channel_id=1, source_target_pairs={{0,8},{8,16},{16,24},{24,32},{32,40},{40,48},{48,56},{56,64},{64,7... | collective-permute-start | bytes 1572872 | tf_op jit(solution)/shard_map/ppermute | solution.py:13
  28.4 611.3 %all-reduce.2.cloned.1.call-start = ((), (), s32[]{:S(2)}) async-start(), calls=%async_computation.2 | async-start | bytes 4718592 | tf_op jit(solution)/shard_map/psum | solution.py:103
  54.7 4.4 copy-start.6
  59.1 54.9 %copy-start.1 = (bf16[1024,256]{1,0:T(8,128)(2,1)S(1)}, bf16[1024,256]{1,0:T(8,128)(2,1)}, u32[]{:S(2)}) copy-start(bf16[1024,256]{1,0:T(8,128)(2,1)} %param.10) | copy-start | bytes 1572868
  62.5 53.8 %copy-start.5 = (bf16[1024,256]{1,0:T(8,128)(2,1)S(1)}, bf16[1024,256]{1,0:T(8,128)(2,1)}, u32[]{:S(2)}) copy-start(bf16[1024,256]{1,0:T(8,128)(2,1)} %param.11) | copy-start | bytes 1572868
  114.0 1.7 copy-start
  122.7 7.4 %copy-start.3 = (f32[512,1536]{0,1:T(8,128)S(1)}, f32[512,1536]{0,1:T(8,128)}, u32[]{:S(2)}) copy-start(f32[512,1536]{0,1:T(8,128)} %get-tuple-element.18) | copy-start | bytes 9437188
  130.1 2.9 copy-start.2
  642.5 2.9 copy-start.7
  644.3 1.0 copy-start.4
  645.4 2.3 copy-start.8
  647.7 7.4 %copy-start.9 = (f32[1,256]{1,0:T(1,128)S(1)}, f32[1,256]{1,0:T(1,128)}, u32[]{:S(2)}) copy-start(f32[1,256]{1,0:T(1,128)} %param.17) | copy-start | bytes 3076
Sparse Core Ops, SparseCore 0:
  11.8 102.1 all-gather.2
  117.8 76.5 all-gather.4
  197.0 442.5 all-reduce.1
where the time goes:
time: 664 us
  waiting for transfers between devices  578 us (87%)
  matrix products  26.9 us (4%)
  other arithmetic  19.6 us (3%)
  starting transfers between devices  18.1 us (3%)
  between operations  14.7 us (2%)
  local copies, waits for them, and re-layouts  6.85 us (1%)
    psum x1, waiting for transfers between devices, local(): total = lax.psum(grad, 'ctx')  445 us
    all_gather x1, waiting for transfers between devices, local(): lax.all_gather(momentum.astype(jnp.bfloat16), 'ctx', axis=3, tiled=True)  58.5 us
    all_gather x1, waiting for transfers between devices, local(): lax.all_gather(fast_weights.astype(jnp.bfloat16), 'ctx', axis=3, tiled=True)  51.5 us
    ppermute x3, waiting for transfers between devices, from_behind(): return lax.ppermute(block, axis, route)  22.2 us
    ppermute x3, starting transfers between devices, from_behind(): return lax.ppermute(block, axis, route)  18 us
  transfers between devices with their start and end apart: 6, of which 4 were waited for; matrix products, arithmetic and copies ran while one was open for 5% of the time, Pallas kernels for 0%

commit v1 on v0

v1 whole, which is shorter than its diff:
```python
import functools
import math

import jax
import jax.numpy as jnp
from jax import lax
from jax.experimental import pallas as pl
from jax.experimental.pallas import tpu as pltpu
from jax.sharding import PartitionSpec as P

DH = 256
HID = 768
TOK = 1024
SHARE = 24
PAIR = 48
TOKENS = 32768
BLK = 256
NBLK = TOK // BLK
MESH = pl.DeviceIdType.MESH
SCALE = math.log2(math.e) / 16.0
NEG = -1e30
F32 = jnp.float32
BF16 = jnp.bfloat16

ZW, ZM, ZG, HDOC = 0, 1, 2, 3
HK, HV = 4, 8
AG1, RS, AG2 = 12, 24, 36
NSEM = 48


def dot_nn(a, b):
    return jnp.dot(a, b, preferred_element_type=F32)


def dot_nt(a, b):
    return lax.dot_general(a, b, (((1,), (1,)), ((), ())), preferred_element_type=F32)


def kernel(
    win_ref, q_ref, k_ref, v_ref, rate_ref, doc_ref, w_ref, m_ref, gain_ref,
    out_ref, nw_ref, nm_ref,
    kt, dp, dpt, kh, vh, doch, dcol,
    wz, mz, wzr, mzr, wp, mp,
    wall, wnew, grad, rs1, rs2s, rs2, tot, totb, totz, nwp, nmp,
    acc, m_s, l_s, normed,
    ssem, rsem,
):
    c, h = lax.axis_index("ctx"), lax.axis_index("head")
    y, x, zh = c // 8, (c // 2) % 4, c % 2
    zpeer = c + 1 - 2 * zh
    nxt, prv = (c + 1) % 32, (c + 31) % 32
    other = (c + 31 + 2 * zh) % 32
    xpeer = [y * 8 + ((x + d) % 4) * 2 + zh for d in (1, 2, 3)]
    ypeer = [((y + d) % 4) * 8 + x * 2 + zh for d in (1, 2, 3)]

    barrier = pltpu.get_barrier_semaphore()
    for peer in [zpeer, other] + xpeer + ypeer:
        pl.semaphore_signal(barrier, inc=1, device_id=(peer, h), device_id_type=MESH)

    def rcopy(src, dst, num, ctx):
        return pltpu.make_async_remote_copy(
            src_ref=src, dst_ref=dst, send_sem=ssem.at[num], recv_sem=rsem.at[num],
            device_id=(ctx, h), device_id_type=MESH,
        )

    started = []

    def start(src, dst, num, ctx):
        copy = rcopy(src, dst, num, ctx)
        copy.start()
        started.append(copy)
        return copy

    own = pl.ds(pl.multiple_of(zh * SHARE, 8), SHARE)
    far = pl.ds(pl.multiple_of((1 - zh) * SHARE, 8), SHARE)
    pad = jnp.zeros((8, DH), F32)
    shares = []
    for ref, full, sent in ((w_ref, wp, wz), (m_ref, mp, mz)):
        rows = [ref[j].T for j in range(3)]
        for j in range(3):
            full[j, own, :] = rows[j]
        sent[...] = jnp.concatenate(rows + [pad], axis=0).astype(BF16)

    pl.semaphore_wait(barrier, 8)
    cw = start(wz, wzr, ZW, zpeer)
    cm = start(mz, mzr, ZM, zpeer)
    hdoc = start(doc_ref, doch, HDOC, nxt)
    halo = {}
    for b in reversed(range(NBLK)):
        rows = pl.ds(b * BLK, BLK)
        halo[b] = (
            start(k_ref.at[rows], kh.at[rows], HK + b, nxt),
            start(v_ref.at[rows], vh.at[rows], HV + b, nxt),
        )

    def gather_first(buf, base):
        return [
            start(buf.at[0, :, y, x], buf.at[0, :, y, x], base + d, xpeer[d]) for d in range(3)
        ] + [
            start(buf.at[1, :, y, x], buf.at[1, :, y, x], base + 3 + d, ypeer[d]) for d in range(3)
        ]

    def gather_second(buf, base, first):
        for copy in first[:3]:
            copy.wait_recv()
        copies = [
            start(buf.at[0, :, y], buf.at[0, :, y], base + 6 + d, ypeer[d]) for d in range(3)
        ]
        for copy in first[3:]:
            copy.wait_recv()
        copies += [
            start(buf.at[1, :, :, x], buf.at[1, :, :, x], base + 9 + d, xpeer[d])
            for d in range(3)
        ]
        return copies

    def set_pair(buf, value):
        value = value.astype(BF16)
        buf[0, :, y, x] = value[:, :, :128]
        buf[1, :, y, x] = value[:, :, 128:]

    def matrix(buf, j):
        return jnp.concatenate(
            [buf[0, j].reshape(HID, 128), buf[1, j].reshape(HID, 128)], axis=-1
        )

    kt[...] = k_ref[...].T
    pred = (-(rate_ref[...] / TOKENS) * v_ref[...].astype(F32)).astype(BF16)
    dp[...] = pred
    dpt[...] = pred.T
    dcol[...] = jnp.broadcast_to(doc_ref[...].astype(F32), (128, TOK)).T

    cw.wait_recv()
    got = wzr[...].astype(F32)
    for j in range(3):
        wp[j, far, :] = got[j * SHARE : (j + 1) * SHARE]
    set_pair(wall, wp[...])
    first = gather_first(wall, AG1)

    window = win_ref[0]

    def attend_own(b):
        n = (b + 1) * BLK
        rows = pl.ds(b * BLK, BLK)
        scores = dot_nn(q_ref[rows, :], kt[:, :n])
        qpos = b * BLK + lax.broadcasted_iota(jnp.int32, (BLK, 1), 0)
        kpos = lax.broadcasted_iota(jnp.int32, (1, n), 1)
        allowed = (kpos <= qpos) & (kpos > qpos - window)
        allowed = allowed & (doc_ref[:, :n].astype(F32) == dcol[rows, 0:1])
        scores = jnp.where(allowed, scores, NEG)
        top = jnp.max(scores, axis=-1, keepdims=True)
        expo = jnp.exp2((scores - top) * SCALE)
        m_s[rows, :] = top
        l_s[rows, :] = jnp.sum(expo, axis=-1, keepdims=True)
        acc[rows, :] = dot_nn(expo.astype(BF16), v_ref[:n, :])

    def attend_halo(b):
        for copy in halo[b]:
            copy.wait_recv()
        krows = pl.ds(b * BLK, BLK)
        keys, values = kh[krows, :], vh[krows, :]
        kdoc = doch[:, b * BLK : (b + 1) * BLK].astype(F32)
        reach = jnp.where(c == 0, -4 * TOK, window)

        def body(i, carry):
            rows = pl.ds(pl.multiple_of(i * BLK, BLK), BLK)
            scores = dot_nt(q_ref[rows, :], keys)
            qpos = i * BLK + lax.broadcasted_iota(jnp.int32, (BLK, 1), 0)
            kpos = b * BLK - TOK + lax.broadcasted_iota(jnp.int32, (1, BLK), 1)
            allowed = (kpos > qpos - reach) & (kdoc == dcol[rows, 0:1])
            scores = jnp.where(allowed, scores, NEG)
            old = m_s[rows, :]
            top = jnp.maximum(old, jnp.max(scores, axis=-1, keepdims=True))
            expo = jnp.exp2((scores - top) * SCALE)
            alpha = jnp.exp2((old - top) * SCALE)
            m_s[rows, :] = top
            l_s[rows, :] = l_s[rows, :] * alpha + jnp.sum(expo, axis=-1, keepdims=True)
            acc[rows, :] = acc[rows, :] * alpha + dot_nn(expo.astype(BF16), values)
            return carry

        lax.fori_loop(0, b + 1, body, 0)

    attend_own(0)
    attend_own(1)
    second = gather_second(wall, AG1, first)
    attend_own(2)
    attend_own(3)
    cm.wait_recv()
    got = mzr[...].astype(F32)
    for j in range(3):
        mp[j, far, :] = got[j * SHARE : (j + 1) * SHARE]
    for copy in second:
        copy.wait_recv()

    def update(yy, carry):
        def part(j):
            return jnp.concatenate(
                [wall[0, j, yy].reshape(192, 128), wall[1, j, yy].reshape(192, 128)], axis=-1
            )

        gate = dot_nn(part(0), kt[...])
        up = dot_nn(part(1), kt[...])
        back = dot_nn(part(2), dpt[...])
        sig = 0.5 * jnp.tanh(0.5 * gate) + 0.5
        active = gate * sig
        hidden = (active * up).astype(BF16)
        d_gate = (back * up * (sig + active * (1.0 - sig))).astype(BF16)
        d_up = (back * active).astype(BF16)
        for j, g in enumerate(
            (dot_nn(d_gate, k_ref[...]), dot_nn(d_up, k_ref[...]), dot_nn(hidden, dp[...]))
        ):
            g = g.astype(BF16).reshape(4, PAIR, DH)
            grad[0, j, yy] = g[:, :, :128]
            grad[1, j, yy] = g[:, :, 128:]
        return carry

    lax.fori_loop(0, 4, update, 0)

    r1a = [
        start(grad.at[0, :, (y + d + 1) % 4], rs1.at[0, d], RS + d, ypeer[d]) for d in range(3)
    ]
    r1b = [
        start(grad.at[1, :, :, (x + d + 1) % 4], rs1.at[1, d], RS + 3 + d, xpeer[d])
        for d in range(3)
    ]
    for copy in r1a:
        copy.wait_recv()
    rs2s[0] = sum([rs1[0, d].astype(F32) for d in range(3)], grad[0, :, y].astype(F32)).astype(
        BF16
    )
    r2a = [
        start(rs2s.at[0, :, (x + d + 1) % 4], rs2.at[0, d], RS + 6 + d, xpeer[d]) for d in range(3)
    ]
    for copy in r1b:
        copy.wait_recv()
    rs2s[1] = sum(
        [rs1[1, d].astype(F32) for d in range(3)], grad[1, :, :, x].astype(F32)
    ).astype(BF16)
    r2b = [
        start(rs2s.at[1, :, (y + d + 1) % 4], rs2.at[1, d], RS + 9 + d, ypeer[d]) for d in range(3)
    ]
    for copy in r2a:
        copy.wait_recv()
    tot[:, :, :128] = sum([rs2[0, d].astype(F32) for d in range(3)], rs2s[0, :, x].astype(F32))
    for copy in r2b:
        copy.wait_recv()
    tot[:, :, 128:] = sum([rs2[1, d].astype(F32) for d in range(3)], rs2s[1, :, y].astype(F32))
    totb[...] = tot[...].astype(BF16)
    cz = start(totb, totz, ZG, zpeer)
    hdoc.wait_recv()
    cz.wait_recv()

    weights = wp[...]
    moment = 0.9 * mp[...] + (tot[...] + totz[...].astype(F32))
    stepped = weights - moment
    factor = jnp.sqrt(jnp.mean(weights * weights, axis=-1, keepdims=True)) / jnp.sqrt(
        jnp.mean(stepped * stepped, axis=-1, keepdims=True) + 1e-06
    )
    fresh = stepped * factor
    set_pair(wnew, fresh)
    first = gather_first(wnew, AG2)
    nwp[...] = fresh
    nmp[...] = moment
    for j in range(3):
        nw_ref[j] = nwp[j, own, :].T
        nm_ref[j] = nmp[j, own, :].T
    second = gather_second(wnew, AG2, first)
    attend_halo(3)
    for copy in second:
        copy.wait_recv()

    new_gate, new_up, new_down = matrix(wnew, 0), matrix(wnew, 1), matrix(wnew, 2)
    gain = gain_ref[...]
    for b in range(NBLK):
        rows = pl.ds(b * BLK, BLK)
        gate = dot_nt(q_ref[rows, :], new_gate)
        up = dot_nt(q_ref[rows, :], new_up)
        sig = 0.5 * jnp.tanh(0.5 * gate) + 0.5
        fast = dot_nn((gate * sig * up).astype(BF16), new_down)
        mean = jnp.mean(fast * fast, axis=-1, keepdims=True)
        normed[rows, :] = fast * lax.rsqrt(mean + 1e-06) * gain

    for b in (2, 1, 0):
        attend_halo(b)
    for b in range(NBLK):
        rows = pl.ds(b * BLK, BLK)
        out_ref[rows, :] = (acc[rows, :] / l_s[rows, :] + normed[rows, :]).astype(BF16)
    for copy in started:
        copy.wait_send()


def local(queries, keys, values, rates, doc_ids, windows, fast_weights, momentum, out_gain):
    vmem = pl.BlockSpec(memory_space=pltpu.VMEM)
    smem = pl.BlockSpec(memory_space=pltpu.SMEM)
    plane = (2, 3, 4, 4, PAIR, 128)
    mixed, new_w, new_m = pl.pallas_call(
        kernel,
        out_shape=(
            jax.ShapeDtypeStruct((TOK, DH), BF16),
            jax.ShapeDtypeStruct((3, DH, SHARE), F32),
            jax.ShapeDtypeStruct((3, DH, SHARE), F32),
        ),
        in_specs=[smem] + [vmem] * 8,
        out_specs=(vmem, vmem, vmem),
        scratch_shapes=[
            pltpu.VMEM((DH, TOK), BF16),
            pltpu.VMEM((TOK, DH), BF16),
            pltpu.VMEM((DH, TOK), BF16),
            pltpu.VMEM((TOK, DH), BF16),
            pltpu.VMEM((TOK, DH), BF16),
            pltpu.VMEM((1, TOK), jnp.int32),
            pltpu.VMEM((TOK, 128), F32),
            pltpu.VMEM((80, DH), BF16),
            pltpu.VMEM((80, DH), BF16),
            pltpu.VMEM((80, DH), BF16),
            pltpu.VMEM((80, DH), BF16),
            pltpu.VMEM((3, PAIR, DH), F32),
            pltpu.VMEM((3, PAIR, DH), F32),
            pltpu.VMEM(plane, BF16),
            pltpu.VMEM(plane, BF16),
            pltpu.VMEM(plane, BF16),
            pltpu.VMEM((2, 3, 3, 4, PAIR, 128), BF16),
            pltpu.VMEM((2, 3, 4, PAIR, 128), BF16),
            pltpu.VMEM((2, 3, 3, PAIR, 128), BF16),
            pltpu.VMEM((3, PAIR, DH), F32),
            pltpu.VMEM((3, PAIR, DH), BF16),
            pltpu.VMEM((3, PAIR, DH), BF16),
            pltpu.VMEM((3, PAIR, DH), F32),
            pltpu.VMEM((3, PAIR, DH), F32),
            pltpu.VMEM((TOK, DH), F32),
            pltpu.VMEM((TOK, 1), F32),
            pltpu.VMEM((TOK, 1), F32),
            pltpu.VMEM((TOK, DH), F32),
            pltpu.SemaphoreType.DMA((NSEM,)),
            pltpu.SemaphoreType.DMA((NSEM,)),
        ],
        compiler_params=pltpu.CompilerParams(
            collective_id=0, has_side_effects=True, vmem_limit_bytes=56 * 2**20
        ),
        name="ttt_layer",
    )(
        windows,
        queries,
        keys,
        values,
        rates,
        doc_ids.reshape(1, TOK),
        fast_weights.reshape(3, DH, SHARE),
        momentum.reshape(3, DH, SHARE),
        out_gain,
    )
    return mixed, new_w.reshape(3, 1, DH, SHARE), new_m.reshape(3, 1, DH, SHARE)


def solution(mesh):
    in_specs = (
        P("ctx", "head"),
        P("ctx", "head"),
        P("ctx", "head"),
        P("ctx", "head"),
        P("ctx"),
        P("head"),
        P(None, "head", None, "ctx"),
        P(None, "head", None, "ctx"),
        P("head", None),
    )
    out_specs = (P("ctx", "head"), P(None, "head", None, "ctx"), P(None, "head", None, "ctx"))
    return jax.shard_map(local, mesh=mesh, in_specs=in_specs, out_specs=out_specs, check_vma=False)
```

time: 664 us -> 101 us (0.15)
  the two profiles are of different devices: /device:TPU:64 before, /device:TPU:224 now
where the time goes in v1:
time: 101 us; the launch traced here: 100 us
  Pallas kernels  90.9 us (90%)
  local copies, waits for them, and re-layouts  8.18 us (8%)
  between operations  1.31 us (1%)
    pallas_call x1, Pallas kernels, local(): pl.pallas_call(kernel, out_shape=(jax.ShapeDtypeStruct((TOK, DH), BF16),...  90.9 us
    unnamed x12, local copies, waits for them, and re-layouts  8.18 us

profile of v1, /device:TPU:224, one launch (start us, length us, event | category | flops | bytes accessed | tf_op | source)
XLA Modules:
  0.0 100.4 jit_solution(14086044634733024475)
XLA Ops:
  1.3 0.0 copy-start.1
  1.3 1.8 %copy.12 = f32[3,1,256,24]{3,2,0,1:T(8,128)} copy(f32[3,1,256,24]{2,3,1,0:T(8,128)} %param.15) | data formatting | bytes 147456 | tf_op args[6]
  3.1 0.0 copy-done.1
  3.1 0.0 copy-start.2
  3.1 0.9 copy.13
  4.1 0.0 copy-done.2
  4.1 1.0 %copy.14.rate_ref = f32[1024,1]{1,0:T(8,128)} copy(f32[1024,1]{0,1:T(1,128)S(1)} %copy-done.2) | data formatting | bytes 8192 | tf_op args[3]
  5.1 90.9 %ttt_layer.1 = (bf16[1024,256]{1,0:T(8,128)(2,1)}, f32[3,256,24]{2,1,0:T(8,128)}, f32[3,256,24]{2,1,0:T(8,128)}) custom-call(s32[1]{0:T(128)S(6)} %copy.18.win_ref, bf16[1024,256]{1,0:T(8,128)(2,1)} %q_ref.1, bf16[1024,256]{1,0:T(8,128)(2,1)} %k_ref.1, bf16[1024,256]{1,0:T(8,128)(2,1)} %v_ref.1, f32[1024,1]{1,0:T(8,128)} %copy.14.rate_ref, ...), custom_call_target="tpu_custom_call" | custom-call | tf_op jit(solution)/shard_map/ttt_layer/pallas_call | solution.py:296
  96.0 0.0 copy-start
  96.0 1.8 %copy.15 = f32[3,1,256,24]{2,3,1,0:T(8,128)} copy(f32[3,1,256,24]{3,2,0,1:T(8,128)} %bitcast.8) | data formatting | bytes 147456
  97.8 1.8 %copy.16 = f32[3,1,256,24]{2,3,1,0:T(8,128)} copy(f32[3,1,256,24]{3,2,0,1:T(8,128)} %bitcast.7) | data formatting | bytes 147456
  99.6 0.0 copy-done
  99.6 0.8 copy.19
Async XLA Ops:
  1.3 1.8 %copy-start.1 = (f32[3,1,256,24]{2,3,1,0:T(8,128)S(1)}, f32[3,1,256,24]{2,3,1,0:T(8,128)}, u32[]{:S(2)}) copy-start(f32[3,1,256,24]{2,3,1,0:T(8,128)} %param.16) | copy-start | bytes 221188
  3.1 0.9 copy-start.2
  96.0 3.6 %copy-start = (bf16[1024,256]{1,0:T(8,128)(2,1)S(1)}, bf16[1024,256]{1,0:T(8,128)(2,1)}, u32[]{:S(2)}) copy-start(bf16[1024,256]{1,0:T(8,128)(2,1)} %get-tuple-element.15) | copy-start | bytes 1572868

commit v2 on v1

--- a/solution.py
+++ b/solution.py
@@ -19,13 +19,14 @@
 MESH = pl.DeviceIdType.MESH
 SCALE = math.log2(math.e) / 16.0
 NEG = -1e30
+SENDS = ((0, 4), (4, 6), (6, 8))
 F32 = jnp.float32
 BF16 = jnp.bfloat16
 
-ZW, ZM, ZG, HDOC = 0, 1, 2, 3
-HK, HV = 4, 8
-AG1, RS, AG2 = 12, 24, 36
-NSEM = 48
+ZW, ZM, HDOC, ZG = 0, 1, 2, 3
+HK, HV = 5, 9
+AG1, RS, AG2 = 13, 25, 37
+NSEM = 49
 
 
 def dot_nn(a, b):
@@ -76,7 +77,7 @@
     pad = jnp.zeros((8, DH), F32)
     shares = []
     for ref, full, sent in ((w_ref, wp, wz), (m_ref, mp, mz)):
-        rows = [ref[j].T for j in range(3)]
+        rows = [ref[j] for j in range(3)]
         for j in range(3):
             full[j, own, :] = rows[j]
         sent[...] = jnp.concatenate(rows + [pad], axis=0).astype(BF16)
@@ -85,13 +86,14 @@
     cw = start(wz, wzr, ZW, zpeer)
     cm = start(mz, mzr, ZM, zpeer)
     hdoc = start(doc_ref, doch, HDOC, nxt)
-    halo = {}
-    for b in reversed(range(NBLK)):
-        rows = pl.ds(b * BLK, BLK)
-        halo[b] = (
-            start(k_ref.at[rows], kh.at[rows], HK + b, nxt),
-            start(v_ref.at[rows], vh.at[rows], HV + b, nxt),
-        )
+    order = [(b, kv) for b in reversed(range(NBLK)) for kv in (0, 1)]
+    halo = {b: [] for b in range(NBLK)}
+
+    def send_halo(first, last):
+        for b, kv in order[first:last]:
+            rows = pl.ds(b * BLK, BLK)
+            src, dst, num = ((k_ref, kh, HK), (v_ref, vh, HV))[kv]
+            halo[b].append(start(src.at[rows], dst.at[rows], num + b, nxt))
 
     def gather_first(buf, base):
         return [
@@ -125,17 +127,10 @@
         )
 
     kt[...] = k_ref[...].T
-    pred = (-(rate_ref[...] / TOKENS) * v_ref[...].astype(F32)).astype(BF16)
-    dp[...] = pred
-    dpt[...] = pred.T
+    pred = (-(rate_ref[...] / TOKENS) * v_ref[...].T.astype(F32)).astype(BF16)
+    dpt[...] = pred
+    dp[...] = pred.T
     dcol[...] = jnp.broadcast_to(doc_ref[...].astype(F32), (128, TOK)).T
-
-    cw.wait_recv()
-    got = wzr[...].astype(F32)
-    for j in range(3):
-        wp[j, far, :] = got[j * SHARE : (j + 1) * SHARE]
-    set_pair(wall, wp[...])
-    first = gather_first(wall, AG1)
 
     window = win_ref[0]
 
@@ -182,8 +177,15 @@
 
     attend_own(0)
     attend_own(1)
+    cw.wait_recv()
+    got = wzr[...].astype(F32)
+    for j in range(3):
+        wp[j, far, :] = got[j * SHARE : (j + 1) * SHARE]
+    set_pair(wall, wp[...])
+    first = gather_first(wall, AG1)
+    send_halo(*SENDS[0])
+    attend_own(2)
     second = gather_second(wall, AG1, first)
-    attend_own(2)
     attend_own(3)
     cm.wait_recv()
     got = mzr[...].astype(F32)
@@ -192,7 +194,9 @@
     for copy in second:
         copy.wait_recv()
 
-    def update(yy, carry):
+    def update(d, carry):
+        yy = (y + 1 + d) % 4
+
         def part(j):
             return jnp.concatenate(
                 [wall[0, j, yy].reshape(192, 128), wall[1, j, yy].reshape(192, 128)], axis=-1
@@ -212,17 +216,28 @@
             g = g.astype(BF16).reshape(4, PAIR, DH)
             grad[0, j, yy] = g[:, :, :128]
             grad[1, j, yy] = g[:, :, 128:]
+
+        @pl.when(d < 3)
+        def _():
+            rcopy(grad.at[0, :, yy], rs1.at[0, d], RS + d, yy * 8 + x * 2 + zh).start()
+
+        for e in range(3):
+            rcopy(
+                grad.at[1, :, yy, (x + e + 1) % 4], rs1.at[1, e, :, yy], RS + 3 + e, xpeer[e]
+            ).start()
         return carry
 
     lax.fori_loop(0, 4, update, 0)
 
     r1a = [
-        start(grad.at[0, :, (y + d + 1) % 4], rs1.at[0, d], RS + d, ypeer[d]) for d in range(3)
+        rcopy(grad.at[0, :, (y + d + 1) % 4], rs1.at[0, d], RS + d, ypeer[d]) for d in range(3)
     ]
     r1b = [
-        start(grad.at[1, :, :, (x + d + 1) % 4], rs1.at[1, d], RS + 3 + d, xpeer[d])
+        rcopy(grad.at[1, :, :, (x + d + 1) % 4], rs1.at[1, d], RS + 3 + d, xpeer[d])
         for d in range(3)
     ]
+    started.extend(r1a + r1b)
+    send_halo(*SENDS[1])
     for copy in r1a:
         copy.wait_recv()
     rs2s[0] = sum([rs1[0, d].astype(F32) for d in range(3)], grad[0, :, y].astype(F32)).astype(
@@ -239,19 +254,24 @@
     r2b = [
         start(rs2s.at[1, :, (y + d + 1) % 4], rs2.at[1, d], RS + 9 + d, ypeer[d]) for d in range(3)
     ]
-    for copy in r2a:
-        copy.wait_recv()
-    tot[:, :, :128] = sum([rs2[0, d].astype(F32) for d in range(3)], rs2s[0, :, x].astype(F32))
-    for copy in r2b:
-        copy.wait_recv()
-    tot[:, :, 128:] = sum([rs2[1, d].astype(F32) for d in range(3)], rs2s[1, :, y].astype(F32))
-    totb[...] = tot[...].astype(BF16)
-    cz = start(totb, totz, ZG, zpeer)
+    cz = []
+    for half, copies, mine in ((0, r2a, x), (1, r2b, y)):
+        lanes = slice(half * 128, half * 128 + 128)
+        for copy in copies:
+            copy.wait_recv()
+        value = sum([rs2[half, d].astype(F32) for d in range(3)], rs2s[half, :, mine].astype(F32))
+        tot[:, :, lanes] = value
+        totb[half] = value.astype(BF16)
+        cz.append(start(totb.at[half], totz.at[half], ZG + half, zpeer))
+    send_halo(*SENDS[2])
     hdoc.wait_recv()
-    cz.wait_recv()
+    attend_halo(3)
+    for copy in cz:
+        copy.wait_recv()
+    tot[...] += jnp.concatenate([totz[0], totz[1]], axis=-1).astype(F32)
 
     weights = wp[...]
-    moment = 0.9 * mp[...] + (tot[...] + totz[...].astype(F32))
+    moment = 0.9 * mp[...] + tot[...]
     stepped = weights - moment
     factor = jnp.sqrt(jnp.mean(weights * weights, axis=-1, keepdims=True)) / jnp.sqrt(
         jnp.mean(stepped * stepped, axis=-1, keepdims=True) + 1e-06
@@ -262,10 +282,10 @@
     nwp[...] = fresh
     nmp[...] = moment
     for j in range(3):
-        nw_ref[j] = nwp[j, own, :].T
-        nm_ref[j] = nmp[j, own, :].T
+        nw_ref[j] = nwp[j, own, :]
+        nm_ref[j] = nmp[j, own, :]
     second = gather_second(wnew, AG2, first)
-    attend_halo(3)
+    attend_halo(2)
     for copy in second:
         copy.wait_recv()
 
@@ -280,7 +300,7 @@
         mean = jnp.mean(fast * fast, axis=-1, keepdims=True)
         normed[rows, :] = fast * lax.rsqrt(mean + 1e-06) * gain
 
-    for b in (2, 1, 0):
+    for b in (1, 0):
         attend_halo(b)
     for b in range(NBLK):
         rows = pl.ds(b * BLK, BLK)
@@ -296,9 +316,9 @@
     mixed, new_w, new_m = pl.pallas_call(
         kernel,
         out_shape=(
-            jax.ShapeDtypeStruct((TOK, DH), BF16),
-            jax.ShapeDtypeStruct((3, DH, SHARE), F32),
-            jax.ShapeDtypeStruct((3, DH, SHARE), F32),
+            pltpu.VMEM((TOK, DH), BF16),
+            pltpu.VMEM((3, SHARE, DH), F32),
+            pltpu.VMEM((3, SHARE, DH), F32),
         ),
         in_specs=[smem] + [vmem] * 8,
         out_specs=(vmem, vmem, vmem),
@@ -323,8 +343,8 @@
             pltpu.VMEM((2, 3, 4, PAIR, 128), BF16),
             pltpu.VMEM((2, 3, 3, PAIR, 128), BF16),
             pltpu.VMEM((3, PAIR, DH), F32),
-            pltpu.VMEM((3, PAIR, DH), BF16),
-            pltpu.VMEM((3, PAIR, DH), BF16),
+            pltpu.VMEM((2, 3, PAIR, 128), BF16),
+            pltpu.VMEM((2, 3, PAIR, 128), BF16),
             pltpu.VMEM((3, PAIR, DH), F32),
             pltpu.VMEM((3, PAIR, DH), F32),
             pltpu.VMEM((TOK, DH), F32),
@@ -343,13 +363,16 @@
         queries,
         keys,
         values,
-        rates,
+        rates.reshape(1, TOK),
         doc_ids.reshape(1, TOK),
-        fast_weights.reshape(3, DH, SHARE),
-        momentum.reshape(3, DH, SHARE),
+        fast_weights.reshape(3, DH, SHARE).transpose(0, 2, 1),
+        momentum.reshape(3, DH, SHARE).transpose(0, 2, 1),
         out_gain,
     )
-    return mixed, new_w.reshape(3, 1, DH, SHARE), new_m.reshape(3, 1, DH, SHARE)
+    new_w, new_m = (
+        part.transpose(0, 2, 1).reshape(3, 1, DH, SHARE) for part in (new_w, new_m)
+    )
+    return mixed, new_w, new_m
 
 
 def solution(mesh):

time: 101 us -> 84.7 us (0.84)
  the two profiles are of different devices: /device:TPU:224 before, /device:TPU:64 now
where the time goes in v2:
time: 84.7 us; the launch traced here: 84.6 us
  Pallas kernels  81.2 us (96%)
  local copies, waits for them, and re-layouts  2.06 us (2%)
  between operations  1.29 us (2%)
    pallas_call x1, Pallas kernels, local(): pl.pallas_call(kernel, out_shape=(pltpu.VMEM((TOK, DH), BF16), pltpu.VMEM...  81.2 us
    unnamed x3, local copies, waits for them, and re-layouts  2.06 us

profile of v2, /device:TPU:64, one launch (start us, length us, event | category | flops | bytes accessed | tf_op | source)
XLA Modules:
  0.0 84.6 jit_solution(2692948731548396918)
XLA Ops:
  1.3 81.2 %ttt_layer.1 = (bf16[1024,256]{1,0:T(8,128)(2,1)S(1)}, f32[3,24,256]{2,1,0:T(8,128)S(1)}, f32[3,24,256]{2,1,0:T(8,128)S(1)}) custom-call(s32[1]{0:T(128)S(6)} %copy.20.win_ref, bf16[1024,256]{1,0:T(8,128)(2,1)} %q_ref.1, bf16[1024,256]{1,0:T(8,128)(2,1)} %k_ref.1, bf16[1024,256]{1,0:T(8,128)(2,1)} %v_ref.1, f32[1,1024]{1,0:T(1,128)} %bitcast.22, ...), custom_call_target="tpu_custom_call" | custom-call | tf_op jit(solution)/shard_map/ttt_layer/pallas_call | solution.py:316
  82.5 0.8 copy.17
  83.3 0.6 copy.18
  84.0 0.6 copy.19

commit v3 on v2

--- a/solution.py
+++ b/solution.py
@@ -19,7 +19,7 @@
 MESH = pl.DeviceIdType.MESH
 SCALE = math.log2(math.e) / 16.0
 NEG = -1e30
-SENDS = ((0, 4), (4, 6), (6, 8))
+SENDS = ((0, 6), (6, 6), (6, 8))
 F32 = jnp.float32
 BF16 = jnp.bfloat16
 
@@ -97,22 +97,22 @@
 
     def gather_first(buf, base):
         return [
-            start(buf.at[0, :, y, x], buf.at[0, :, y, x], base + d, xpeer[d]) for d in range(3)
+            start(buf.at[0, :, y, x], buf.at[0, :, y, x], base + d, xpeer[d]) for d in (1, 0, 2)
         ] + [
-            start(buf.at[1, :, y, x], buf.at[1, :, y, x], base + 3 + d, ypeer[d]) for d in range(3)
+            start(buf.at[1, :, y, x], buf.at[1, :, y, x], base + 3 + d, ypeer[d]) for d in (1, 0, 2)
         ]
 
     def gather_second(buf, base, first):
         for copy in first[:3]:
             copy.wait_recv()
         copies = [
-            start(buf.at[0, :, y], buf.at[0, :, y], base + 6 + d, ypeer[d]) for d in range(3)
+            start(buf.at[0, :, y], buf.at[0, :, y], base + 6 + d, ypeer[d]) for d in (1, 0, 2)
         ]
         for copy in first[3:]:
             copy.wait_recv()
         copies += [
             start(buf.at[1, :, :, x], buf.at[1, :, :, x], base + 9 + d, xpeer[d])
-            for d in range(3)
+            for d in (1, 0, 2)
         ]
         return copies
 

time: 84.7 us -> 83.3 us (0.983)
  Pallas kernels: 81.2 us -> 79.3 us
    pallas_call x1, Pallas kernels: 81.2 us -> 79.3 us  [local(): pl.pallas_call(kernel, out_shape=(pltpu.VMEM((TOK, DH), BF16), pltpu.VMEM...]
where the time goes in v3:
time: 83.3 us; the launch traced here: 82.6 us
  Pallas kernels  79.3 us (95%)
  local copies, waits for them, and re-layouts  2.06 us (2%)
  between operations  1.29 us (2%)
    pallas_call x1, Pallas kernels, local(): pl.pallas_call(kernel, out_shape=(pltpu.VMEM((TOK, DH), BF16), pltpu.VMEM...  79.3 us
    unnamed x3, local copies, waits for them, and re-layouts  2.06 us

profile of v3, /device:TPU:64, one launch (start us, length us, event | category | flops | bytes accessed | tf_op | source)
XLA Modules:
  0.0 82.6 jit_solution(5429228766670594409)
XLA Ops:
  1.3 79.3 %ttt_layer.1 = (bf16[1024,256]{1,0:T(8,128)(2,1)S(1)}, f32[3,24,256]{2,1,0:T(8,128)S(1)}, f32[3,24,256]{2,1,0:T(8,128)S(1)}) custom-call(s32[1]{0:T(128)S(6)} %copy.20.win_ref, bf16[1024,256]{1,0:T(8,128)(2,1)} %q_ref.1, bf16[1024,256]{1,0:T(8,128)(2,1)} %k_ref.1, bf16[1024,256]{1,0:T(8,128)(2,1)} %v_ref.1, f32[1,1024]{1,0:T(1,128)} %bitcast.22, ...), custom_call_target="tpu_custom_call" | custom-call | tf_op jit(solution)/shard_map/ttt_layer/pallas_call | solution.py:316
  80.5 0.8 copy.17
  81.3 0.6 copy.18
  82.0 0.6 copy.19

commit v4 on v3

--- a/solution.py
+++ b/solution.py
@@ -300,11 +300,15 @@
         mean = jnp.mean(fast * fast, axis=-1, keepdims=True)
         normed[rows, :] = fast * lax.rsqrt(mean + 1e-06) * gain
 
+    def finish(b):
+        rows = pl.ds(b * BLK, BLK)
+        out_ref[rows, :] = (acc[rows, :] / l_s[rows, :] + normed[rows, :]).astype(BF16)
+
+    finish(3)
+    finish(2)
     for b in (1, 0):
         attend_halo(b)
-    for b in range(NBLK):
-        rows = pl.ds(b * BLK, BLK)
-        out_ref[rows, :] = (acc[rows, :] / l_s[rows, :] + normed[rows, :]).astype(BF16)
+        finish(b)
     for copy in started:
         copy.wait_send()
 

time: 83.3 us -> 83.4 us (level)
  no operation moved by 1% of the time
where the time goes in v4:
time: 83.4 us; the launch traced here: 82.7 us
  Pallas kernels  79.3 us (95%)
  local copies, waits for them, and re-layouts  2.06 us (2%)
  between operations  1.29 us (2%)
    pallas_call x1, Pallas kernels, local(): pl.pallas_call(kernel, out_shape=(pltpu.VMEM((TOK, DH), BF16), pltpu.VMEM...  79.3 us
    unnamed x3, local copies, waits for them, and re-layouts  2.06 us

profile of v4, /device:TPU:64, one launch (start us, length us, event | category | flops | bytes accessed | tf_op | source)
XLA Modules:
  0.0 82.7 jit_solution(10225379768295087286)
XLA Ops:
  1.3 79.3 %ttt_layer.1 = (bf16[1024,256]{1,0:T(8,128)(2,1)S(1)}, f32[3,24,256]{2,1,0:T(8,128)S(1)}, f32[3,24,256]{2,1,0:T(8,128)S(1)}) custom-call(s32[1]{0:T(128)S(6)} %copy.20.win_ref, bf16[1024,256]{1,0:T(8,128)(2,1)} %q_ref.1, bf16[1024,256]{1,0:T(8,128)(2,1)} %k_ref.1, bf16[1024,256]{1,0:T(8,128)(2,1)} %v_ref.1, f32[1,1024]{1,0:T(1,128)} %bitcast.22, ...), custom_call_target="tpu_custom_call" | custom-call | tf_op jit(solution)/shard_map/ttt_layer/pallas_call | solution.py:320
  80.6 0.8 copy.17
  81.4 0.6 copy.18
  82.0 0.6 copy.19
